TPU v7x, 256 devices: a whole 4x4x8 slice. The times are simulated.
256 devices in a mesh: outer: 16 (over y_hi, z), inner: 16 (over y_lo, x, core).
Axes of the slice: x: 4, y: 4 (y_hi: 2, y_lo: 2; y = y_hi * 2 + y_lo), z: 8, core: 2. Of those that a mesh axis runs over, the one named last changes fastest.
Arguments:
- queries: bfloat16 [65536, 2048], P(('outer', 'inner')), may hold values from -64 to 64
- keys: bfloat16 [65536, 2048], P(('outer', 'inner')), may hold values from -6 to 6
- values: bfloat16 [65536, 2048], P(('outer', 'inner')), may hold values from -6 to 6
- level_blocks: int32 [512, 4], P(('outer', 'inner')), may hold values from -1 to 507, as said below
- global_blocks: int32 [8], replicated, may hold values from 0 to 127, as said below
Outputs:
- attended: bfloat16 [65536, 2048], P(('outer', 'inner'))
Inputs may be any that keep to these rules, and one draw needn't show every extreme that they name: level_blocks[b, j] is -1 exactly when b // 2 < 2 ** (j + 1); otherwise it is one of the 2 blocks of group b // 2 - 2 ** (j + 1). `global_blocks`: the global summary blocks are distinct.
All inputs are finite; a program needn't handle non-finite values.
Results may differ from a plain program's by a relative error of at most 0.0042.
Values may be sent and summed in bfloat16 or wider, within the bound.
A program may use at most 128 MiB of HBM per device.

v0:
```python
import math

import jax
import jax.numpy as jnp
from jax import lax
from jax.sharding import PartitionSpec as P

H = 16
DH = 128
BLK = 128


masked_score = -1e30


def passed_along(value, axis, steps):
    count = lax.axis_size(axis)
    first, last = (max(0, -steps), min(count, count - steps))
    return lax.ppermute(value, axis, [(source, source + steps) for source in range(first, last)])


def spread(value, axis, source):
    kept = jnp.where(lax.axis_index(axis) == source, value, 0).astype(value.dtype)
    return lax.psum(kept, axis)


def head_scores(query_heads, key_rows, score_scale):
    key_heads = key_rows.reshape(key_rows.shape[0], query_heads.shape[1], query_heads.shape[2])
    return (
        jnp.einsum("qhd,khd->hqk", query_heads, key_heads, preferred_element_type=jnp.float32)
        * score_scale
    )


def head_values(weights, value_rows, query_heads):
    value_heads = value_rows.reshape(
        value_rows.shape[0], query_heads.shape[1], query_heads.shape[2]
    )
    return jnp.einsum(
        "hqk,khd->qhd",
        weights.astype(jnp.bfloat16),
        value_heads,
        preferred_element_type=jnp.float32,
    )


def shards(queries, keys, values, level_blocks, global_blocks):
    tok_rows, width = queries.shape
    blocks = tok_rows // BLK
    head_count = H
    n_inner = lax.axis_size("inner")
    device = lax.axis_index("outer") * n_inner + lax.axis_index("inner")
    score_scale = 1.0 / math.sqrt(DH)
    level_count = level_blocks.shape[1]
    prev_keys, prev_values = passed_along((keys, values), ("outer", "inner"), 1)
    far_keys = []
    far_values = []
    for level_step in range(level_count):
        moved = passed_along((keys, values), ("outer", "inner"), 2 ** (level_step + 1))
        far_keys.append(moved[0])
        far_values.append(moved[1])
    picked_keys = []
    picked_values = []
    live_flags = []
    for level_step in range(level_count):
        wanted = level_blocks[:, level_step]
        is_live = wanted >= 0
        source_group = device - 2 ** (level_step + 1)
        slot_index = jnp.where(is_live, wanted - source_group * blocks, 0)
        picked_keys.append(far_keys[level_step].reshape(blocks, BLK, width)[slot_index])
        picked_values.append(far_values[level_step].reshape(blocks, BLK, width)[slot_index])
        live_flags.append(is_live)
    level_keys = jnp.stack(picked_keys, axis=1).reshape(blocks, level_count * BLK, width)
    level_values = jnp.stack(picked_values, axis=1).reshape(blocks, level_count * BLK, width)
    level_live = jnp.repeat(jnp.stack(live_flags, axis=1), BLK, axis=1)
    own_keys = keys.reshape(blocks, BLK, width)
    own_values = values.reshape(blocks, BLK, width)
    summary_keys = []
    summary_values = []
    for glob_step in range(global_blocks.shape[0]):
        target_block = global_blocks[glob_step]
        owner_index = target_block // blocks
        slot_index = target_block % blocks
        own_piece = (
            lax.dynamic_index_in_dim(own_keys, slot_index, 0, keepdims=False),
            lax.dynamic_index_in_dim(own_values, slot_index, 0, keepdims=False),
        )
        received = (
            spread(own_piece[0], ("outer", "inner"), owner_index),
            spread(own_piece[1], ("outer", "inner"), owner_index),
        )
        summary_keys.append(received[0])
        summary_values.append(received[1])
    glob_keys = jnp.concatenate(summary_keys, axis=0)
    glob_values = jnp.concatenate(summary_values, axis=0)
    near_keys = jnp.concatenate([prev_keys, keys], axis=0)
    near_values = jnp.concatenate([prev_values, values], axis=0)
    key_pos = jnp.arange(2 * tok_rows, dtype=jnp.int32) - tok_rows
    later_group = device > 0
    row_offsets = jnp.arange(BLK, dtype=jnp.int32)
    glob_pos = (global_blocks[:, None] * BLK + row_offsets[None, :]).reshape(-1)
    device_start = device * tok_rows

    def attend(inputs):
        block_index, query_rows, lev_keys, lev_values, lev_live = inputs
        query_heads = query_rows.reshape(BLK, head_count, width // head_count)
        query_pos = block_index * BLK + row_offsets
        near_allowed = (key_pos[None, :] <= query_pos[:, None]) & (
            (key_pos[None, :] >= 0) | later_group
        )
        glob_allowed = glob_pos[None, :] <= (device_start + query_pos)[:, None]
        near_scores = jnp.where(
            near_allowed[None], head_scores(query_heads, near_keys, score_scale), masked_score
        )
        level_scores = jnp.where(
            lev_live[None, None, :], head_scores(query_heads, lev_keys, score_scale), masked_score
        )
        glob_scores = jnp.where(
            glob_allowed[None], head_scores(query_heads, glob_keys, score_scale), masked_score
        )
        row_max = jnp.maximum(
            jnp.maximum(
                jnp.max(near_scores, axis=-1, keepdims=True),
                jnp.max(level_scores, axis=-1, keepdims=True),
            ),
            jnp.max(glob_scores, axis=-1, keepdims=True),
        )
        near_weights = jnp.exp(near_scores - row_max)
        level_weights = jnp.exp(level_scores - row_max)
        glob_weights = jnp.exp(glob_scores - row_max)
        row_total = (
            jnp.sum(near_weights, axis=-1, keepdims=True)
            + jnp.sum(level_weights, axis=-1, keepdims=True)
            + jnp.sum(glob_weights, axis=-1, keepdims=True)
        )
        summed = (
            head_values(near_weights, near_values, query_heads)
            + head_values(level_weights, lev_values, query_heads)
            + head_values(glob_weights, glob_values, query_heads)
        )
        result = summed / jnp.transpose(row_total, (1, 0, 2))
        return result.reshape(BLK, width).astype(jnp.bfloat16)

    outputs = lax.map(
        attend,
        (
            jnp.arange(blocks, dtype=jnp.int32),
            queries.reshape(blocks, BLK, width),
            level_keys,
            level_values,
            level_live,
        ),
    )
    return outputs.reshape(tok_rows, width)


def solution(mesh):
    placed = (
        P(("outer", "inner"), None),
        P(("outer", "inner"), None),
        P(("outer", "inner"), None),
        P(("outer", "inner"), None),
        P(),
    )
    return jax.shard_map(
        shards, mesh=mesh, in_specs=placed, out_specs=P(("outer", "inner"), None), check_vma=False
    )
```

profile of v0, /device:TPU:17, one launch (start us, length us, event | category | flops | bytes accessed | tf_op | source)
XLA Modules:
  0.0 599.9 jit_solution(9601999327547146341)
XLA Ops:
  6.5 1.6 fusion.66
  28.5 4.5 select_bitcast_fusion
  33.0 2.1 select_bitcast_fusion.8
  35.1 1.2 copy-done.2
  36.3 3.1 collective-permute-start.6
  39.4 4.4 collective-permute-start.7
  43.8 2.9 collective-permute-start.8
  46.7 3.5 collective-permute-start.9
  50.3 3.0 collective-permute-start.1
  54.1 67.8 %collective-permute-done.6 = bf16[256,2048]{1,0:T(8,128)(2,1)} collective-permute-done((bf16[256,2048]{1,0:T(8,128)(2,1)S(1)}, bf16[256,2048]{1,0:T(8,128)(2,1)}, u32[]{:S(2)}, u32[]{:S(2)}) %collective-permute-start.6) | collective-permute-done | bytes 1048608 | tf_op jit(solution)/shard_map/ppermute | solution.py:19
  121.9 1.9 collective-permute-start.2
  123.9 8.9 %collective-permute-done.7 = bf16[256,2048]{1,0:T(8,128)(2,1)} collective-permute-done((bf16[256,2048]{1,0:T(8,128)(2,1)S(1)}, bf16[256,2048]{1,0:T(8,128)(2,1)}, u32[]{:S(2)}, u32[]{:S(2)}) %collective-permute-start.7) | collective-permute-done | bytes 1048608 | tf_op jit(solution)/shard_map/ppermute | solution.py:19
  132.8 1.9 collective-permute-start.3
  134.7 25.3 %collective-permute-done.8 = bf16[256,2048]{1,0:T(8,128)(2,1)} collective-permute-done((bf16[256,2048]{1,0:T(8,128)(2,1)S(1)}, bf16[256,2048]{1,0:T(8,128)(2,1)}, u32[]{:S(2)}, u32[]{:S(2)}) %collective-permute-start.8) | collective-permute-done | bytes 1048608 | tf_op jit(solution)/shard_map/ppermute | solution.py:19
  160.0 2.5 collective-permute-start.4
  162.6 1.9 collective-permute-start.5
  164.6 76.5 %collective-permute-done.1 = bf16[256,2048]{1,0:T(8,128)(2,1)} collective-permute-done((bf16[256,2048]{1,0:T(8,128)(2,1)S(1)}, bf16[256,2048]{1,0:T(8,128)(2,1)}, u32[]{:S(2)}, u32[]{:S(2)}) %collective-permute-start.1) | collective-permute-done | bytes 1048608 | tf_op jit(solution)/shard_map/ppermute | solution.py:19
  241.1 1.9 collective-permute-start
  243.1 1.9 gather_fusion.4
  244.9 2.8 gather_fusion.5
  247.8 2.8 gather_fusion.6
  250.6 2.9 gather_fusion.7
  253.5 2.2 pad_maximum_fusion.1
  255.7 2.3 copy.44
  258.0 1.9 gather_fusion
  259.9 2.9 gather_fusion.1
  262.7 2.9 gather_fusion.2
  265.6 2.8 gather_fusion.3
  268.4 2.1 pad_maximum_fusion
  270.6 2.3 copy.41
  272.8 2.8 pad_maximum_fusion.3
  275.6 2.7 pad_maximum_fusion.2
  278.4 214.7 %all-reduce.3.cloned.1.call-done = (bf16[128,2048]{1,0:T(8,128)(2,1)}, bf16[128,2048]{1,0:T(8,128)(2,1)}, bf16[128,2048]{1,0:T(8,128)(2,1)}, bf16[128,2048]{1,0:...) async-done(((bf16[128,2048]{1,0:T(8,128)(2,1)}, ...) | async-done | bytes 8388624 | tf_op jit(solution)/shard_map/psum | solution.py:24
  493.1 2.1 constant_dynamic-update-slice_fusion.16
  495.1 2.0 constant_dynamic-update-slice_fusion.8
  497.1 2.0 constant_dynamic-update-slice_fusion.15
  499.1 2.0 constant_dynamic-update-slice_fusion.14
  509.5 1.1 constant_dynamic-update-slice_fusion.1
  510.6 6.4 %copy.48 = bf16[1024,2048]{0,1:T(8,128)(2,1)} copy(bf16[1024,2048]{1,0:T(8,128)(2,1)} %get-tuple-element.305) | data formatting | bytes 8388608
  517.0 76.0 %while.12 = (s32[]{:T(128)}, bf16[2,128,2048]{2,1,0:T(8,128)(2,1)}, s32[2]{0:T(128)S(1)}, pred[]{:T(512)}, bf16[2,128,2048]{2,1,0:T(8,128)(2,1)}, /*index=5*/bf1...) while((s32[]{:T(128)}, bf16[2,128,2048]{2,1,0:T(8,128)(2,1)}, ...), condition=%wide.region_23.24_spmd.clone.clone, body=%wide.region_16.23_spmd.clone.clone.sunk | while | flops 2194930944 | bytes 154060688 | solution.py:144
  517.0 4.0 constant_dynamic-slice_fusion.6
  521.0 3.9 copy.85
  524.9 1.1 constant_dynamic-slice_fusion.5
  526.3 2.5 fusion.109
  530.4 4.1 fusion.107
  534.7 1.3 fusion.108
  535.9 2.4 fusion.113
  538.3 2.3 fusion.112
  540.6 2.4 fusion.111
  543.0 3.6 fusion.110
  546.6 2.5 copy.86
  549.1 4.6 divide_convert_fusion.2
  555.0 4.0 constant_dynamic-slice_fusion.6
  559.0 3.9 copy.85
  562.9 1.1 constant_dynamic-slice_fusion.5
  564.3 2.5 fusion.109
  568.4 4.1 fusion.107
  572.7 1.3 fusion.108
  574.0 2.4 fusion.113
  576.3 2.3 fusion.112
  578.6 2.4 fusion.111
  581.0 3.6 fusion.110
  584.6 2.5 copy.86
  587.2 4.6 divide_convert_fusion.2
  (111 shorter events, 14.7 us)
Async XLA Ops:
  6.5 486.5 %all-reduce.3.cloned.1.call-start = ((), (), s32[]{:S(2)}) async-start(), calls=%async_computation | async-start | bytes 16777216 | tf_op jit(solution)/shard_map/psum | solution.py:24
  28.5 4.5 copy-start.3
  35.1 1.2 copy-start.2
  35.1 18.8 %copy-start.19 = (s32[2,4]{1,0:T(2,128)S(1)}, s32[2,4]{1,0:T(2,128)}, u32[]{:S(2)}) copy-start(s32[2,4]{1,0:T(2,128)} %param.10) | copy-start | bytes 100
  35.1 129.5 %copy-start.18 = (s32[8]{0:T(128)S(1)}, s32[8]{0:T(128)}, u32[]{:S(2)}) copy-start(s32[8]{0:T(128)} %param.11) | copy-start | bytes 100
  36.3 85.7 %collective-permute-start.6 = (bf16[256,2048]{1,0:T(8,128)(2,1)S(1)}, bf16[256,2048]{1,0:T(8,128)(2,1)}, u32[]{:S(2)}, u32[]{:S(2)}) collective-permute-start(bf16[256,2048]{1,0:T(8,128)(2,1)S(1)} %copy-done.2), channel_id=1, source_target_pairs={{0,2},{1,3},{2,4},{3,5},{4,6},{5,7},{6,8},{7,9},{8,10},{9,11},{10,... | collective-permute-start | bytes 3145736 | tf_op jit(solution)/shard_map/ppermute | solution.py:19
  39.4 93.4 %collective-permute-start.7 = (bf16[256,2048]{1,0:T(8,128)(2,1)S(1)}, bf16[256,2048]{1,0:T(8,128)(2,1)}, u32[]{:S(2)}, u32[]{:S(2)}) collective-permute-start(bf16[256,2048]{1,0:T(8,128)(2,1)S(1)} %copy-done.2), channel_id=1, source_target_pairs={{0,4},{1,5},{2,6},{3,7},{4,8},{5,9},{6,10},{7,11},{8,12},{9,13},{1... | collective-permute-start | bytes 3145736 | tf_op jit(solution)/shard_map/ppermute | solution.py:19
  43.8 116.2 %collective-permute-start.8 = (bf16[256,2048]{1,0:T(8,128)(2,1)S(1)}, bf16[256,2048]{1,0:T(8,128)(2,1)}, u32[]{:S(2)}, u32[]{:S(2)}) collective-permute-start(bf16[256,2048]{1,0:T(8,128)(2,1)S(1)} %copy-done.2), channel_id=1, source_target_pairs={{0,8},{1,9},{2,10},{3,11},{4,12},{5,13},{6,14},{7,15},{8,16},{9,17... | collective-permute-start | bytes 3145736 | tf_op jit(solution)/shard_map/ppermute | solution.py:19
  46.7 116.0 %collective-permute-start.9 = (bf16[256,2048]{1,0:T(8,128)(2,1)S(1)}, bf16[256,2048]{1,0:T(8,128)(2,1)}, u32[]{:S(2)}, u32[]{:S(2)}) collective-permute-start(bf16[256,2048]{1,0:T(8,128)(2,1)S(1)} %copy-done.2), channel_id=1, source_target_pairs={{0,16},{1,17},{2,18},{3,19},{4,20},{5,21},{6,22},{7,23},{8,24},{9,... | collective-permute-start | bytes 3145736 | tf_op jit(solution)/shard_map/ppermute | solution.py:19
  50.3 190.9 %collective-permute-start.1 = (bf16[256,2048]{1,0:T(8,128)(2,1)S(1)}, bf16[256,2048]{1,0:T(8,128)(2,1)}, u32[]{:S(2)}, u32[]{:S(2)}) collective-permute-start(bf16[256,2048]{1,0:T(8,128)(2,1)S(1)} %copy-done.3), channel_id=1, source_target_pairs={{0,2},{1,3},{2,4},{3,5},{4,6},{5,7},{6,8},{7,9},{8,10},{9,11},{10,... | collective-permute-start | bytes 3145736 | tf_op jit(solution)/shard_map/ppermute | solution.py:19
  121.9 137.9 %collective-permute-start.2 = (bf16[256,2048]{1,0:T(8,128)(2,1)S(1)}, bf16[256,2048]{1,0:T(8,128)(2,1)}, u32[]{:S(2)}, u32[]{:S(2)}) collective-permute-start(bf16[256,2048]{1,0:T(8,128)(2,1)S(1)} %copy-done.3), channel_id=1, source_target_pairs={{0,4},{1,5},{2,6},{3,7},{4,8},{5,9},{6,10},{7,11},{8,12},{9,13},{1... | collective-permute-start | bytes 3145736 | tf_op jit(solution)/shard_map/ppermute | solution.py:19
  132.8 129.9 %collective-permute-start.3 = (bf16[256,2048]{1,0:T(8,128)(2,1)S(1)}, bf16[256,2048]{1,0:T(8,128)(2,1)}, u32[]{:S(2)}, u32[]{:S(2)}) collective-permute-start(bf16[256,2048]{1,0:T(8,128)(2,1)S(1)} %copy-done.3), channel_id=1, source_target_pairs={{0,8},{1,9},{2,10},{3,11},{4,12},{5,13},{6,14},{7,15},{8,16},{9,17... | collective-permute-start | bytes 3145736 | tf_op jit(solution)/shard_map/ppermute | solution.py:19
  160.0 105.6 %collective-permute-start.4 = (bf16[256,2048]{1,0:T(8,128)(2,1)S(1)}, bf16[256,2048]{1,0:T(8,128)(2,1)}, u32[]{:S(2)}, u32[]{:S(2)}) collective-permute-start(bf16[256,2048]{1,0:T(8,128)(2,1)S(1)} %copy-done.3), channel_id=1, source_target_pairs={{0,16},{1,17},{2,18},{3,19},{4,20},{5,21},{6,22},{7,23},{8,24},{9,... | collective-permute-start | bytes 3145736 | tf_op jit(solution)/shard_map/ppermute | solution.py:19
  162.6 110.2 %collective-permute-start.5 = (bf16[256,2048]{0,1:T(8,128)(2,1)S(1)}, bf16[256,2048]{0,1:T(8,128)(2,1)}, u32[]{:S(2)}, u32[]{:S(2)}) collective-permute-start(bf16[256,2048]{0,1:T(8,128)(2,1)S(1)} %copy.42), channel_id=1, source_target_pairs={{0,1},{1,2},{2,3},{3,4},{4,5},{5,6},{6,7},{7,8},{8,9},{9,10},{10,1... | collective-permute-start | bytes 3145736 | tf_op jit(solution)/shard_map/ppermute | solution.py:19
  241.1 34.5 %collective-permute-start = (bf16[256,2048]{1,0:T(8,128)(2,1)S(1)}, bf16[256,2048]{1,0:T(8,128)(2,1)}, u32[]{:S(2)}, u32[]{:S(2)}) collective-permute-start(bf16[256,2048]{1,0:T(8,128)(2,1)S(1)} %copy-done.3), channel_id=1, source_target_pairs={{0,1},{1,2},{2,3},{3,4},{4,5},{5,6},{6,7},{7,8},{8,9},{9,10},{10,1... | collective-permute-start | bytes 3145736 | tf_op jit(solution)/shard_map/ppermute | solution.py:19
  493.0 8.0 %copy-start.15 = (bf16[128,2048]{1,0:T(8,128)(2,1)S(1)}, bf16[128,2048]{1,0:T(8,128)(2,1)}, u32[]{:S(2)}) copy-start(bf16[128,2048]{1,0:T(8,128)(2,1)} %get-tuple-element.261) | copy-start | bytes 1572868
  493.0 8.9 %copy-start.14 = (bf16[128,2048]{1,0:T(8,128)(2,1)S(1)}, bf16[128,2048]{1,0:T(8,128)(2,1)}, u32[]{:S(2)}) copy-start(bf16[128,2048]{1,0:T(8,128)(2,1)} %get-tuple-element.262) | copy-start | bytes 1572868
  493.0 9.7 %copy-start.13 = (bf16[128,2048]{1,0:T(8,128)(2,1)S(1)}, bf16[128,2048]{1,0:T(8,128)(2,1)}, u32[]{:S(2)}) copy-start(bf16[128,2048]{1,0:T(8,128)(2,1)} %get-tuple-element.263) | copy-start | bytes 1572868
  493.0 10.6 %copy-start.12 = (bf16[128,2048]{1,0:T(8,128)(2,1)S(1)}, bf16[128,2048]{1,0:T(8,128)(2,1)}, u32[]{:S(2)}) copy-start(bf16[128,2048]{1,0:T(8,128)(2,1)} %get-tuple-element.264) | copy-start | bytes 1572868
  493.0 11.4 %copy-start.11 = (bf16[128,2048]{1,0:T(8,128)(2,1)S(1)}, bf16[128,2048]{1,0:T(8,128)(2,1)}, u32[]{:S(2)}) copy-start(bf16[128,2048]{1,0:T(8,128)(2,1)} %get-tuple-element.251) | copy-start | bytes 1572868
  495.1 10.2 %copy-start.10 = (bf16[128,2048]{1,0:T(8,128)(2,1)S(1)}, bf16[128,2048]{1,0:T(8,128)(2,1)}, u32[]{:S(2)}) copy-start(bf16[128,2048]{1,0:T(8,128)(2,1)} %get-tuple-element.252) | copy-start | bytes 1572868
  497.1 9.0 %copy-start.9 = (bf16[128,2048]{1,0:T(8,128)(2,1)S(1)}, bf16[128,2048]{1,0:T(8,128)(2,1)}, u32[]{:S(2)}) copy-start(bf16[128,2048]{1,0:T(8,128)(2,1)} %get-tuple-element.253) | copy-start | bytes 1572868
  499.1 7.9 %copy-start.8 = (bf16[128,2048]{1,0:T(8,128)(2,1)S(1)}, bf16[128,2048]{1,0:T(8,128)(2,1)}, u32[]{:S(2)}) copy-start(bf16[128,2048]{1,0:T(8,128)(2,1)} %get-tuple-element.254) | copy-start | bytes 1572868
  501.1 6.8 %copy-start.7 = (bf16[128,2048]{1,0:T(8,128)(2,1)S(1)}, bf16[128,2048]{1,0:T(8,128)(2,1)}, u32[]{:S(2)}) copy-start(bf16[128,2048]{1,0:T(8,128)(2,1)} %get-tuple-element.255) | copy-start | bytes 1572868
  501.9 6.8 %copy-start.6 = (bf16[128,2048]{1,0:T(8,128)(2,1)S(1)}, bf16[128,2048]{1,0:T(8,128)(2,1)}, u32[]{:S(2)}) copy-start(bf16[128,2048]{1,0:T(8,128)(2,1)} %get-tuple-element.256) | copy-start | bytes 1572868
  502.8 6.8 %copy-start.16 = (bf16[128,2048]{1,0:T(8,128)(2,1)S(1)}, bf16[128,2048]{1,0:T(8,128)(2,1)}, u32[]{:S(2)}) copy-start(bf16[128,2048]{1,0:T(8,128)(2,1)} %get-tuple-element.257) | copy-start | bytes 1572868
  502.8 6.8 %copy-start.17 = (bf16[128,2048]{1,0:T(8,128)(2,1)S(1)}, bf16[128,2048]{1,0:T(8,128)(2,1)}, u32[]{:S(2)}) copy-start(bf16[128,2048]{1,0:T(8,128)(2,1)} %get-tuple-element.265) | copy-start | bytes 1572868
  528.8 7.2 %copy-start = (f32[16,128,512]{2,1,0:T(8,128)}, f32[16,128,512]{2,1,0:T(8,128)S(1)}, u32[]{:S(2)}) copy-start(f32[16,128,512]{2,1,0:T(8,128)S(1)} %get-tuple-element.412) | copy-start | bytes 12582916 | tf_op jit(solution)/shard_map/while
  530.4 4.3 copy-start.1
  538.3 2.3 copy-start.5
  540.6 2.4 copy-start.4
  549.1 4.8 copy-start.20
  554.0 1.0 copy-start.21
  566.8 7.2 %copy-start = (f32[16,128,512]{2,1,0:T(8,128)}, f32[16,128,512]{2,1,0:T(8,128)S(1)}, u32[]{:S(2)}) copy-start(f32[16,128,512]{2,1,0:T(8,128)S(1)} %get-tuple-element.412) | copy-start | bytes 12582916 | tf_op jit(solution)/shard_map/while
  568.4 4.3 copy-start.1
  576.3 2.3 copy-start.5
  578.6 2.4 copy-start.4
  587.2 4.8 copy-start.20
  592.1 1.0 copy-start.21
Sparse Core Ops, SparseCore 0:
  35.2 457.7 all-reduce.2
where the time goes:
time: 604 us; the launch traced here: 600 us
  waiting for transfers between devices  393 us (65%)
  local copies, waits for them, and re-layouts  80.3 us (13%)
  matrix products  36.9 us (6%)
  between operations  34 us (6%)
  starting transfers between devices  27.1 us (4%)
  other arithmetic  26.6 us (4%)
    psum x1, waiting for transfers between devices, spread(): return lax.psum(kept, axis)  215 us
    ppermute x10, waiting for transfers between devices, passed_along(): lax.ppermute(value, axis, [(source, source + steps) for source in range(f...  179 us
    ppermute x10, starting transfers between devices, passed_along(): lax.ppermute(value, axis, [(source, source + steps) for source in range(f...  27.1 us
    dynamic_slice x14, local copies, waits for them, and re-layouts, shards(): lax.map(attend, (jnp.arange(blocks, dtype=jnp.int32), queries.reshape(blo...  25.1 us
    unnamed x50, local copies, waits for them, and re-layouts  24.6 us
    dot_general x6, matrix products, head_values(): jnp.einsum('hqk,khd->qhd', weights.astype(jnp.bfloat16), value_heads, pre...  21.2 us
    dot_general x6, matrix products, head_scores(): jnp.einsum('qhd,khd->hqk', query_heads, key_heads, preferred_element_type...  15.7 us
  transfers between devices with their start and end apart: 11, of which 5 were waited for; matrix products, arithmetic and copies ran while one was open for 6% of the time, Pallas kernels for 0%

commit v1 on v0

v1 whole, which is shorter than its diff:
```python
import functools
import math

import jax
import jax.numpy as jnp
from jax import lax
from jax.experimental import pallas as pl
from jax.experimental.pallas import tpu as pltpu
from jax.sharding import PartitionSpec as P

MESH = pl.DeviceIdType.MESH
N = 16
DH = 128
BLK = 128
GRP = 256
LEV = 4
NGLOB = 8
MASKED = -1e30
SCALE_LOG2 = math.log2(math.e) / math.sqrt(DH)


def remote(src, dst, send, recv, device):
    return pltpu.make_async_remote_copy(
        src_ref=src, dst_ref=dst, send_sem=send, recv_sem=recv, device_id=device, device_id_type=MESH
    )


def head_columns(ref, head):
    return ref.at[:, pl.ds(pl.multiple_of(head * DH, DH), DH)]


def dot_keys(rows, keys):
    return lax.dot_general(rows, keys, (((1,), (1,)), ((), ())), preferred_element_type=jnp.float32)


def dot_values(weights, rows):
    return jnp.dot(weights.astype(jnp.bfloat16), rows, preferred_element_type=jnp.float32)


def attend(part, i, qbuf, kv, lbs, gb_ref, gbuf):
    group = part * N + i
    q = qbuf[i]
    row = lax.broadcasted_iota(jnp.int32, (GRP, GRP), 0)
    col = lax.broadcasted_iota(jnp.int32, (GRP, GRP), 1)
    s_prev = jnp.where(group > 0, dot_keys(q, kv[15 + i, 0]), MASKED)
    s_own = jnp.where(col <= row, dot_keys(q, kv[16 + i, 0]), MASKED)
    s_glob = dot_keys(q, gbuf[0:NGLOB].reshape(NGLOB * BLK, DH))
    ahead = (col - row)[:, :BLK]
    s_glob = jnp.concatenate(
        [
            jnp.where(
                ahead <= group * GRP - gb_ref[t] * BLK, s_glob[:, t * BLK : (t + 1) * BLK], MASKED
            )
            for t in range(NGLOB)
        ],
        axis=1,
    )
    s_lev, v_lev = [], []
    for b in range(2):
        keys, vals = [], []
        for j in range(LEV):
            reach = 2 ** (j + 1)
            second = lbs[i, 0, b * LEV + j] == 2 * (group - reach) + 1
            k_pair = kv[16 + i - reach, 0]
            v_pair = kv[16 + i - reach, 1]
            keys.append(jnp.where(second, k_pair[BLK:], k_pair[:BLK]))
            vals.append(jnp.where(second, v_pair[BLK:], v_pair[:BLK]))
        s = dot_keys(q[b * BLK : (b + 1) * BLK], jnp.concatenate(keys, axis=0))
        s_lev.append(
            jnp.concatenate(
                [
                    jnp.where(group >= 2 ** (j + 1), s[:, j * BLK : (j + 1) * BLK], MASKED)
                    for j in range(LEV)
                ],
                axis=1,
            )
        )
        v_lev.append(jnp.concatenate(vals, axis=0))
    s_lev = jnp.concatenate(s_lev, axis=0)
    top = jnp.maximum(
        jnp.maximum(
            jnp.max(s_prev, axis=1, keepdims=True), jnp.max(s_own, axis=1, keepdims=True)
        ),
        jnp.maximum(
            jnp.max(s_glob, axis=1, keepdims=True), jnp.max(s_lev, axis=1, keepdims=True)
        ),
    )
    p_prev = jnp.exp2((s_prev - top) * SCALE_LOG2)
    p_own = jnp.exp2((s_own - top) * SCALE_LOG2)
    p_glob = jnp.exp2((s_glob - top) * SCALE_LOG2)
    p_lev = jnp.exp2((s_lev - top) * SCALE_LOG2)
    total = (
        jnp.sum(p_prev, axis=1, keepdims=True)
        + jnp.sum(p_own, axis=1, keepdims=True)
        + jnp.sum(p_glob, axis=1, keepdims=True)
        + jnp.sum(p_lev, axis=1, keepdims=True)
    )
    acc = (
        dot_values(p_prev, kv[15 + i, 1])
        + dot_values(p_own, kv[16 + i, 1])
        + dot_values(p_glob, gbuf[NGLOB : 2 * NGLOB].reshape(NGLOB * BLK, DH))
        + jnp.concatenate([dot_values(p_lev[:BLK], v_lev[0]), dot_values(p_lev[BLK:], v_lev[1])], axis=0)
    )
    return (acc / total).astype(jnp.bfloat16)


def kernel(
    q_ref, k_ref, v_ref, lb_ref, gb_ref, out_ref,
    qbuf, kv, lbv, lbs, g1src, g1buf, g2src, gbuf, obuf,
    k_send, v_send, q_send, l_send, k_recv, v_recv, q_recv, l_recv,
    h_send, h_recv, g1_send, g1_recv, g2_send, g2_recv, o_send, o_recv, own_sem,
):
    part = lax.axis_index("outer")
    me = lax.axis_index("inner")
    right = lax.rem(part + 1, N)

    barrier = pltpu.get_barrier_semaphore()

    def greet(t, _):
        pl.semaphore_signal(
            barrier, inc=1, device_id=(part, lax.rem(me + t, N)), device_id_type=MESH
        )
        pl.semaphore_signal(
            barrier, inc=1, device_id=(lax.rem(part + t, N), me), device_id_type=MESH
        )
        return 0

    lax.fori_loop(1, N, greet, 0)
    pl.semaphore_wait(barrier, 2 * (N - 1))

    def k_copy(slot, head, device):
        return remote(
            head_columns(k_ref, head), kv.at[16 + slot, 0], k_send.at[head], k_recv.at[slot], device
        )

    def v_copy(slot, head, device):
        return remote(
            head_columns(v_ref, head), kv.at[16 + slot, 1], v_send.at[head], v_recv.at[slot], device
        )

    def q_copy(slot, head, device):
        return remote(
            head_columns(q_ref, head), qbuf.at[slot], q_send.at[head], q_recv.at[slot], device
        )

    def l_copy(slot, head, device):
        return remote(lb_ref, lbv.at[slot], l_send.at[head], l_recv.at[slot], device)

    own_k = pltpu.make_async_copy(head_columns(k_ref, me), kv.at[16 + me, 0], k_recv.at[me])
    own_v = pltpu.make_async_copy(head_columns(v_ref, me), kv.at[16 + me, 1], v_recv.at[me])
    own_q = pltpu.make_async_copy(head_columns(q_ref, me), qbuf.at[me], q_recv.at[me])
    own_l = pltpu.make_async_copy(lb_ref, lbv.at[me], l_recv.at[me])
    own_k.start()
    own_v.start()
    own_q.start()
    own_l.start()

    def send_kv(t, _):
        to = lax.rem(me + t, N)
        k_copy(me, to, (part, to)).start()
        v_copy(me, to, (part, to)).start()
        return 0

    def send_q(t, _):
        to = lax.rem(me + t, N)
        q_copy(me, to, (part, to)).start()
        l_copy(me, to, (part, to)).start()
        return 0

    lax.fori_loop(1, N, send_kv, 0)
    lax.fori_loop(1, N, send_q, 0)

    def halo_copy(slot):
        return remote(
            kv.at[16 + slot], kv.at[slot], h_send.at[slot], h_recv.at[slot], (right, me)
        )

    def forward(n, _):
        slot = lax.rem(8 + n, N)
        k_copy(slot, me, (part, me)).wait_recv()
        v_copy(slot, me, (part, me)).wait_recv()
        halo_copy(slot).start()
        return 0

    lax.fori_loop(0, N, forward, 0)

    def g1_copy(t):
        return remote(g1src.at[t], g1buf.at[part], g1_send.at[t], g1_recv.at[part], (t, me))

    own_g1 = pltpu.make_async_copy(g1src.at[part], g1buf.at[lax.rem(part, 4)], own_sem.at[0])

    @pl.when(part < 4)
    def _():
        for t in range(NGLOB):
            wanted = gb_ref[t] - part * (2 * N)

            def look(slot, found):
                pick_k, pick_v = found
                keys, vals = kv[16 + slot, 0], kv[16 + slot, 1]
                for half in range(2):
                    here = wanted == 2 * slot + half
                    pick_k = jnp.where(here, keys[half * BLK : (half + 1) * BLK], pick_k)
                    pick_v = jnp.where(here, vals[half * BLK : (half + 1) * BLK], pick_v)
                return pick_k, pick_v

            zero = jnp.zeros((BLK, DH), jnp.bfloat16)
            pick_k, pick_v = lax.fori_loop(0, N, look, (zero, zero))
            g1src[2 * t] = pick_k
            g1src[2 * t + 1] = pick_v
        own_g1.start()

        def send_g1(t, _):
            g1_copy_to = lax.rem(part + t, N)
            g1_copy(g1_copy_to).start()
            return 0

        lax.fori_loop(1, N, send_g1, 0)
        own_g1.wait()

    def wait_g1(source, _):
        @pl.when(source != part)
        def _():
            remote(
                g1src.at[0], g1buf.at[source], g1_send.at[0], g1_recv.at[source], (part, me)
            ).wait_recv()

        return 0

    lax.fori_loop(0, 4, wait_g1, 0)
    piece = jnp.zeros((BLK, DH), jnp.bfloat16)
    holder = gb_ref[part // 2] // (2 * N)
    for source in range(4):
        piece = jnp.where(holder == source, g1buf[source], piece)
    g2src[...] = piece

    def g2_place(t):
        return gbuf.at[lax.rem(t, 2) * NGLOB + t // 2]

    def g2_copy(slot, to):
        return remote(g2src, g2_place(slot), g2_send.at[to], g2_recv.at[slot], (to, me))

    own_g2 = pltpu.make_async_copy(g2src, g2_place(part), own_sem.at[1])
    own_g2.start()

    def send_g2(t, _):
        to = lax.rem(part + t, N)
        g2_copy(part, to).start()
        return 0

    lax.fori_loop(1, N, send_g2, 0)

    def wait_q(slot, _):
        q_copy(slot, me, (part, me)).wait_recv()
        l_copy(slot, me, (part, me)).wait_recv()
        return 0

    lax.fori_loop(0, N, wait_q, 0)
    to_scalars = pltpu.make_async_copy(lbv, lbs, own_sem.at[2])
    to_scalars.start()
    to_scalars.wait()

    own_g2.wait()

    def wait_g2(t, _):
        g2_copy(lax.rem(part + t, N), me).wait_recv()
        return 0

    lax.fori_loop(1, N, wait_g2, 0)

    def o_copy(group, head):
        return remote(
            obuf.at[group], head_columns(out_ref, head), o_send.at[group], o_recv.at[head], (part, group)
        )

    own_o = pltpu.make_async_copy(obuf.at[me], head_columns(out_ref, me), own_sem.at[3])

    def step(n, _):
        i = lax.rem(8 + n, N)
        halo_copy(i).wait_recv()
        obuf[i] = attend(part, i, qbuf, kv, lbs, gb_ref, gbuf)

        @pl.when(i == me)
        def _():
            own_o.start()

        @pl.when(i != me)
        def _():
            o_copy(i, me).start()

        return 0

    lax.fori_loop(0, N, step, 0)
    own_o.wait()

    def finish(t, _):
        other = lax.rem(me + t, N)
        k_copy(me, other, (part, other)).wait_send()
        v_copy(me, other, (part, other)).wait_send()
        q_copy(me, other, (part, other)).wait_send()
        l_copy(me, other, (part, other)).wait_send()
        o_copy(other, me).wait_send()
        o_copy(me, other).wait_recv()
        g2_copy(part, lax.rem(part + t, N)).wait_send()
        return 0

    lax.fori_loop(1, N, finish, 0)

    def finish_halo(slot, _):
        halo_copy(slot).wait_send()
        return 0

    lax.fori_loop(0, N, finish_halo, 0)

    @pl.when(part < 4)
    def _():
        def finish_g1(t, _):
            g1_copy(lax.rem(part + t, N)).wait_send()
            return 0

        lax.fori_loop(1, N, finish_g1, 0)


def shards(queries, keys, values, level_blocks, global_blocks):
    rows, width = queries.shape
    levels = jnp.pad(level_blocks.reshape(1, -1), ((0, 7), (0, DH - level_blocks.size)))
    anywhere = pl.BlockSpec(memory_space=pl.ANY)
    sems = pltpu.SemaphoreType.DMA
    return pl.pallas_call(
        kernel,
        out_shape=jax.ShapeDtypeStruct((rows, width), jnp.bfloat16),
        in_specs=[
            anywhere,
            anywhere,
            anywhere,
            pl.BlockSpec(memory_space=pltpu.VMEM),
            pl.BlockSpec(memory_space=pltpu.SMEM),
        ],
        out_specs=anywhere,
        scratch_shapes=[
            pltpu.VMEM((N, GRP, DH), jnp.bfloat16),
            pltpu.VMEM((2 * N, 2, GRP, DH), jnp.bfloat16),
            pltpu.VMEM((N, 8, DH), jnp.int32),
            pltpu.SMEM((N, 8, DH), jnp.int32),
            pltpu.VMEM((N, BLK, DH), jnp.bfloat16),
            pltpu.VMEM((4, BLK, DH), jnp.bfloat16),
            pltpu.VMEM((BLK, DH), jnp.bfloat16),
            pltpu.VMEM((2 * NGLOB, BLK, DH), jnp.bfloat16),
            pltpu.VMEM((N, GRP, DH), jnp.bfloat16),
        ]
        + [sems((N,))] * 8
        + [sems((N,)), sems((N,)), sems((N,)), sems((4,)), sems((N,)), sems((N,)), sems((N,)), sems((N,)), sems((4,))],
        compiler_params=pltpu.CompilerParams(
            collective_id=0, has_side_effects=True, vmem_limit_bytes=40 * 2**20
        ),
        cost_estimate=pl.CostEstimate(
            flops=4 * rows * width * 2048, bytes_accessed=8 * rows * width, transcendentals=rows * 2048 * N
        ),
    )(queries, keys, values, levels, global_blocks)


def solution(mesh):
    placed = P(("outer", "inner"), None)
    return jax.shard_map(
        shards,
        mesh=mesh,
        in_specs=(placed, placed, placed, placed, P()),
        out_specs=placed,
        check_vma=False,
    )
```

time: 604 us -> 188 us (0.31)
  the two profiles are of different devices: /device:TPU:17 before, /device:TPU:7 now
where the time goes in v1:
time: 188 us
  Pallas kernels  182 us (97%)
  local copies, waits for them, and re-layouts  6.06 us (3%)
    pallas_call x1, Pallas kernels, shards(): pl.pallas_call(kernel, out_shape=jax.ShapeDtypeStruct((rows, width), jnp....  182 us
    unnamed x9, local copies, waits for them, and re-layouts  5.29 us

profile of v1, /device:TPU:7, one launch (start us, length us, event | category | flops | bytes accessed | tf_op | source)
XLA Modules:
  0.0 187.9 jit_solution(5607051722267091069)
XLA Ops:
  0.0 0.8 reshape.3
  0.8 0.0 copy-start.3
  0.8 0.6 copy-done.3
  1.4 0.0 copy-start
  1.4 1.2 copy-done
  2.6 0.0 copy-start.1
  2.6 1.2 copy-done.1
  3.9 0.0 copy-start.2
  3.9 1.2 copy-done.2
  5.1 181.8 %shard_map.55 = bf16[256,2048]{1,0:T(8,128)(2,1)S(1)} custom-call(bf16[256,2048]{1,0:T(8,128)(2,1)S(1)} %copy-done, bf16[256,2048]{1,0:T(8,128)(2,1)S(1)} %copy-done.1, bf16[256,2048]{1,0:T(8,128)(2,1)S(1)} %copy-done.2, s32[8,128]{1,0:T(8,128)S(1)} %pad.4.lb_ref, s32[8]{0:T(128)S(1)} %copy-done.3), custom_call_target="tpu_custom_call" | custom-call | flops 4294967296 | bytes 4194304 | tf_op jit(solution)/shard_map/pallas_call | solution.py:328
  186.9 1.0 copy.7
  (1 shorter events, 0.0 us)
Async XLA Ops:
  0.8 0.7 copy-start.3
  1.4 1.2 copy-start
  2.6 1.2 copy-start.1
  3.9 1.2 copy-start.2

commit v2 on v1

--- a/solution.py
+++ b/solution.py
@@ -27,6 +27,10 @@
 
 def head_columns(ref, head):
     return ref.at[:, pl.ds(pl.multiple_of(head * DH, DH), DH)]
+
+
+def head_at(part, inner):
+    return lax.rem(inner + (part // 8) * 8, N)
 
 
 def dot_keys(rows, keys):
@@ -113,6 +117,11 @@
     part = lax.axis_index("outer")
     me = lax.axis_index("inner")
     right = lax.rem(part + 1, N)
+    head = head_at(part, me)
+    right_inner = head_at(right, head)
+
+    def across(other):
+        return (other, head_at(other, head))
 
     barrier = pltpu.get_barrier_semaphore()
 
@@ -121,34 +130,31 @@
             barrier, inc=1, device_id=(part, lax.rem(me + t, N)), device_id_type=MESH
         )
         pl.semaphore_signal(
-            barrier, inc=1, device_id=(lax.rem(part + t, N), me), device_id_type=MESH
+            barrier, inc=1, device_id=across(lax.rem(part + t, N)), device_id_type=MESH
         )
         return 0
 
     lax.fori_loop(1, N, greet, 0)
     pl.semaphore_wait(barrier, 2 * (N - 1))
 
-    def k_copy(slot, head, device):
-        return remote(
-            head_columns(k_ref, head), kv.at[16 + slot, 0], k_send.at[head], k_recv.at[slot], device
-        )
-
-    def v_copy(slot, head, device):
-        return remote(
-            head_columns(v_ref, head), kv.at[16 + slot, 1], v_send.at[head], v_recv.at[slot], device
-        )
-
-    def q_copy(slot, head, device):
-        return remote(
-            head_columns(q_ref, head), qbuf.at[slot], q_send.at[head], q_recv.at[slot], device
-        )
-
-    def l_copy(slot, head, device):
-        return remote(lb_ref, lbv.at[slot], l_send.at[head], l_recv.at[slot], device)
-
-    own_k = pltpu.make_async_copy(head_columns(k_ref, me), kv.at[16 + me, 0], k_recv.at[me])
-    own_v = pltpu.make_async_copy(head_columns(v_ref, me), kv.at[16 + me, 1], v_recv.at[me])
-    own_q = pltpu.make_async_copy(head_columns(q_ref, me), qbuf.at[me], q_recv.at[me])
+    def k_copy(source, to):
+        columns = head_columns(k_ref, head_at(part, to))
+        return remote(columns, kv.at[16 + source, 0], k_send.at[to], k_recv.at[source], (part, to))
+
+    def v_copy(source, to):
+        columns = head_columns(v_ref, head_at(part, to))
+        return remote(columns, kv.at[16 + source, 1], v_send.at[to], v_recv.at[source], (part, to))
+
+    def q_copy(source, to):
+        columns = head_columns(q_ref, head_at(part, to))
+        return remote(columns, qbuf.at[source], q_send.at[to], q_recv.at[source], (part, to))
+
+    def l_copy(source, to):
+        return remote(lb_ref, lbv.at[source], l_send.at[to], l_recv.at[source], (part, to))
+
+    own_k = pltpu.make_async_copy(head_columns(k_ref, head), kv.at[16 + me, 0], k_recv.at[me])
+    own_v = pltpu.make_async_copy(head_columns(v_ref, head), kv.at[16 + me, 1], v_recv.at[me])
+    own_q = pltpu.make_async_copy(head_columns(q_ref, head), qbuf.at[me], q_recv.at[me])
     own_l = pltpu.make_async_copy(lb_ref, lbv.at[me], l_recv.at[me])
     own_k.start()
     own_v.start()
@@ -157,35 +163,50 @@
 
     def send_kv(t, _):
         to = lax.rem(me + t, N)
-        k_copy(me, to, (part, to)).start()
-        v_copy(me, to, (part, to)).start()
-        return 0
-
-    def send_q(t, _):
-        to = lax.rem(me + t, N)
-        q_copy(me, to, (part, to)).start()
-        l_copy(me, to, (part, to)).start()
+        k_copy(me, to).start()
+        v_copy(me, to).start()
         return 0
 
     lax.fori_loop(1, N, send_kv, 0)
-    lax.fori_loop(1, N, send_q, 0)
+
+    @pl.when(part == 0)
+    def _():
+        def blank(slot, _):
+            kv[slot] = jnp.zeros((2, GRP, DH), jnp.bfloat16)
+            return 0
+
+        lax.fori_loop(0, N, blank, 0)
 
     def halo_copy(slot):
         return remote(
-            kv.at[16 + slot], kv.at[slot], h_send.at[slot], h_recv.at[slot], (right, me)
+            kv.at[16 + slot], kv.at[slot], h_send.at[slot], h_recv.at[slot], (right, right_inner)
         )
 
-    def forward(n, _):
-        slot = lax.rem(8 + n, N)
-        k_copy(slot, me, (part, me)).wait_recv()
-        v_copy(slot, me, (part, me)).wait_recv()
-        halo_copy(slot).start()
-        return 0
-
-    lax.fori_loop(0, N, forward, 0)
+    own_k.wait()
+    own_v.wait()
+
+    @pl.when(part < N - 1)
+    def _():
+        halo_copy(me).start()
+
+    def forward(t, _):
+        slot = lax.rem(me + N - t, N)
+        k_copy(slot, me).wait_recv()
+        v_copy(slot, me).wait_recv()
+
+        @pl.when(part < N - 1)
+        def _():
+            halo_copy(slot).start()
+
+        to = lax.rem(me + t, N)
+        q_copy(me, to).start()
+        l_copy(me, to).start()
+        return 0
+
+    lax.fori_loop(1, N, forward, 0)
 
     def g1_copy(t):
-        return remote(g1src.at[t], g1buf.at[part], g1_send.at[t], g1_recv.at[part], (t, me))
+        return remote(g1src.at[t], g1buf.at[part], g1_send.at[t], g1_recv.at[part], across(t))
 
     own_g1 = pltpu.make_async_copy(g1src.at[part], g1buf.at[lax.rem(part, 4)], own_sem.at[0])
 
@@ -237,7 +258,7 @@
         return gbuf.at[lax.rem(t, 2) * NGLOB + t // 2]
 
     def g2_copy(slot, to):
-        return remote(g2src, g2_place(slot), g2_send.at[to], g2_recv.at[slot], (to, me))
+        return remote(g2src, g2_place(slot), g2_send.at[to], g2_recv.at[slot], across(to))
 
     own_g2 = pltpu.make_async_copy(g2src, g2_place(part), own_sem.at[1])
     own_g2.start()
@@ -249,12 +270,16 @@
 
     lax.fori_loop(1, N, send_g2, 0)
 
-    def wait_q(slot, _):
-        q_copy(slot, me, (part, me)).wait_recv()
-        l_copy(slot, me, (part, me)).wait_recv()
-        return 0
-
-    lax.fori_loop(0, N, wait_q, 0)
+    own_q.wait()
+    own_l.wait()
+
+    def wait_q(t, _):
+        slot = lax.rem(me + N - t, N)
+        q_copy(slot, me).wait_recv()
+        l_copy(slot, me).wait_recv()
+        return 0
+
+    lax.fori_loop(1, N, wait_q, 0)
     to_scalars = pltpu.make_async_copy(lbv, lbs, own_sem.at[2])
     to_scalars.start()
     to_scalars.wait()
@@ -262,31 +287,50 @@
     own_g2.wait()
 
     def wait_g2(t, _):
-        g2_copy(lax.rem(part + t, N), me).wait_recv()
+        g2_copy(lax.rem(part + t, N), part).wait_recv()
         return 0
 
     lax.fori_loop(1, N, wait_g2, 0)
 
-    def o_copy(group, head):
-        return remote(
-            obuf.at[group], head_columns(out_ref, head), o_send.at[group], o_recv.at[head], (part, group)
-        )
-
-    own_o = pltpu.make_async_copy(obuf.at[me], head_columns(out_ref, me), own_sem.at[3])
-
-    def step(n, _):
-        i = lax.rem(8 + n, N)
-        halo_copy(i).wait_recv()
-        obuf[i] = attend(part, i, qbuf, kv, lbs, gb_ref, gbuf)
-
-        @pl.when(i == me)
+    def o_copy(group, source):
+        columns = head_columns(out_ref, head_at(part, source))
+        return remote(obuf.at[group], columns, o_send.at[group], o_recv.at[source], (part, group))
+
+    own_o = pltpu.make_async_copy(obuf.at[me], head_columns(out_ref, head), own_sem.at[3])
+
+    first = head_at(lax.rem(part + N - 1, N), head)
+
+    def came(slot):
+        return lax.rem(first + N - slot, N)
+
+    def ready(i):
+        last = came(i)
+        for back in (8, 4, 2, 1):
+            other = i + N - back
+            last = jnp.maximum(last, jnp.where(other < N, came(lax.rem(other, N)), 0))
+        return last
+
+    def step(t, _):
+        @pl.when(part > 0)
         def _():
-            own_o.start()
-
-        @pl.when(i != me)
-        def _():
-            o_copy(i, me).start()
-
+            halo_copy(lax.rem(first + N - t, N)).wait_recv()
+
+        def group(i, _):
+            @pl.when(ready(i) == t)
+            def _():
+                obuf[i] = attend(part, i, qbuf, kv, lbs, gb_ref, gbuf)
+
+                @pl.when(i == me)
+                def _():
+                    own_o.start()
+
+                @pl.when(i != me)
+                def _():
+                    o_copy(i, me).start()
+
+            return 0
+
+        lax.fori_loop(0, N, group, 0)
         return 0
 
     lax.fori_loop(0, N, step, 0)
@@ -294,10 +338,10 @@
 
     def finish(t, _):
         other = lax.rem(me + t, N)
-        k_copy(me, other, (part, other)).wait_send()
-        v_copy(me, other, (part, other)).wait_send()
-        q_copy(me, other, (part, other)).wait_send()
-        l_copy(me, other, (part, other)).wait_send()
+        k_copy(me, other).wait_send()
+        v_copy(me, other).wait_send()
+        q_copy(me, other).wait_send()
+        l_copy(me, other).wait_send()
         o_copy(other, me).wait_send()
         o_copy(me, other).wait_recv()
         g2_copy(part, lax.rem(part + t, N)).wait_send()
@@ -305,11 +349,13 @@
 
     lax.fori_loop(1, N, finish, 0)
 
-    def finish_halo(slot, _):
-        halo_copy(slot).wait_send()
-        return 0
-
-    lax.fori_loop(0, N, finish_halo, 0)
+    @pl.when(part < N - 1)
+    def _():
+        def finish_halo(slot, _):
+            halo_copy(slot).wait_send()
+            return 0
+
+        lax.fori_loop(0, N, finish_halo, 0)
 
     @pl.when(part < 4)
     def _():
@@ -350,7 +396,7 @@
         + [sems((N,))] * 8
         + [sems((N,)), sems((N,)), sems((N,)), sems((4,)), sems((N,)), sems((N,)), sems((N,)), sems((N,)), sems((4,))],
         compiler_params=pltpu.CompilerParams(
-            collective_id=0, has_side_effects=True, vmem_limit_bytes=40 * 2**20
+            collective_id=0, has_side_effects=True, vmem_limit_bytes=60 * 2**20
         ),
         cost_estimate=pl.CostEstimate(
             flops=4 * rows * width * 2048, bytes_accessed=8 * rows * width, transcendentals=rows * 2048 * N

time: 188 us -> 129 us (0.69)
  the two profiles are of different devices: /device:TPU:7 before, /device:TPU:17 now
where the time goes in v2:
time: 129 us; the launch traced here: 128 us
  Pallas kernels  124 us (96%)
  local copies, waits for them, and re-layouts  3.66 us (3%)
    pallas_call x1, Pallas kernels, shards(): pl.pallas_call(kernel, out_shape=jax.ShapeDtypeStruct((rows, width), jnp....  124 us

profile of v2, /device:TPU:17, one launch (start us, length us, event | category | flops | bytes accessed | tf_op | source)
XLA Modules:
  0.0 127.6 jit_solution(8726866376806443508)
XLA Ops:
  0.0 0.8 reshape.3
  0.8 0.6 pad.4.lb_ref
  1.4 123.9 %shard_map.55 = bf16[256,2048]{1,0:T(8,128)(2,1)} custom-call(bf16[256,2048]{1,0:T(8,128)(2,1)} %q_ref.1, bf16[256,2048]{1,0:T(8,128)(2,1)} %k_ref.1, bf16[256,2048]{1,0:T(8,128)(2,1)} %v_ref.1, s32[8,128]{1,0:T(8,128)} %pad.4.lb_ref, s32[8]{0:T(128)} %gb_ref.1), custom_call_target="tpu_custom_call" | custom-call | flops 4294967296 | bytes 4194304 | tf_op jit(solution)/shard_map/pallas_call | solution.py:374
  125.3 2.3 %copy.7 = bf16[256,2048]{1,0:T(8,128)(2,1)} copy(bf16[256,2048]{1,0:T(8,128)(2,1)} %shard_map.55) | data formatting | bytes 2097152

commit v3 on v2

--- a/solution.py
+++ b/solution.py
@@ -16,6 +16,9 @@
 LEV = 4
 NGLOB = 8
 MASKED = -1e30
+MOVES = ((2, 0), (1, 0), (3, 1), (0, 0), (2, 1), (1, 1), (3, 0), (0, 1))
+HELD = 3
+FAR_FIRST = (4, 3, 5, 2, 6, 1, 7)
 SCALE_LOG2 = math.log2(math.e) / math.sqrt(DH)
 
 
@@ -33,6 +36,11 @@
     return lax.rem(inner + (part // 8) * 8, N)
 
 
+def moved(inner, dy, dx, dc):
+    y, x, core = inner // 8, inner // 2, inner
+    return lax.rem(y + dy, 2) * 8 + lax.rem(x + dx, 4) * 2 + lax.rem(core + dc, 2)
+
+
 def dot_keys(rows, keys):
     return lax.dot_general(rows, keys, (((1,), (1,)), ((), ())), preferred_element_type=jnp.float32)
 
@@ -41,44 +49,47 @@
     return jnp.dot(weights.astype(jnp.bfloat16), rows, preferred_element_type=jnp.float32)
 
 
-def attend(part, i, qbuf, kv, lbs, gb_ref, gbuf):
+def attend(part, i, masked_far, masked_glob, qbuf, kv, lbs, gb_ref, gbuf):
     group = part * N + i
     q = qbuf[i]
     row = lax.broadcasted_iota(jnp.int32, (GRP, GRP), 0)
     col = lax.broadcasted_iota(jnp.int32, (GRP, GRP), 1)
-    s_prev = jnp.where(group > 0, dot_keys(q, kv[15 + i, 0]), MASKED)
+    s_prev = dot_keys(q, kv[15 + i, 0])
+    if masked_far:
+        s_prev = jnp.where(group > 0, s_prev, MASKED)
     s_own = jnp.where(col <= row, dot_keys(q, kv[16 + i, 0]), MASKED)
     s_glob = dot_keys(q, gbuf[0:NGLOB].reshape(NGLOB * BLK, DH))
-    ahead = (col - row)[:, :BLK]
-    s_glob = jnp.concatenate(
-        [
-            jnp.where(
-                ahead <= group * GRP - gb_ref[t] * BLK, s_glob[:, t * BLK : (t + 1) * BLK], MASKED
-            )
-            for t in range(NGLOB)
-        ],
-        axis=1,
-    )
+    if masked_glob:
+        ahead = (col - row)[:, :BLK]
+        s_glob = jnp.concatenate(
+            [
+                jnp.where(
+                    ahead <= group * GRP - gb_ref[t] * BLK, s_glob[:, t * BLK : (t + 1) * BLK], MASKED
+                )
+                for t in range(NGLOB)
+            ],
+            axis=1,
+        )
     s_lev, v_lev = [], []
     for b in range(2):
         keys, vals = [], []
         for j in range(LEV):
             reach = 2 ** (j + 1)
-            second = lbs[i, 0, b * LEV + j] == 2 * (group - reach) + 1
+            second = lbs[i, b, j] == 2 * (group - reach) + 1
             k_pair = kv[16 + i - reach, 0]
             v_pair = kv[16 + i - reach, 1]
             keys.append(jnp.where(second, k_pair[BLK:], k_pair[:BLK]))
             vals.append(jnp.where(second, v_pair[BLK:], v_pair[:BLK]))
         s = dot_keys(q[b * BLK : (b + 1) * BLK], jnp.concatenate(keys, axis=0))
-        s_lev.append(
-            jnp.concatenate(
+        if masked_far:
+            s = jnp.concatenate(
                 [
                     jnp.where(group >= 2 ** (j + 1), s[:, j * BLK : (j + 1) * BLK], MASKED)
                     for j in range(LEV)
                 ],
                 axis=1,
             )
-        )
+        s_lev.append(s)
         v_lev.append(jnp.concatenate(vals, axis=0))
     s_lev = jnp.concatenate(s_lev, axis=0)
     top = jnp.maximum(
@@ -112,7 +123,7 @@
     q_ref, k_ref, v_ref, lb_ref, gb_ref, out_ref,
     qbuf, kv, lbv, lbs, g1src, g1buf, g2src, gbuf, obuf,
     k_send, v_send, q_send, l_send, k_recv, v_recv, q_recv, l_recv,
-    h_send, h_recv, g1_send, g1_recv, g2_send, g2_recv, o_send, o_recv, own_sem,
+    h_send, h_recv, g1_send, g1_recv, g2_send, g2_recv, g2_over, o_send, o_recv, own_sem,
 ):
     part = lax.axis_index("outer")
     me = lax.axis_index("inner")
@@ -161,13 +172,12 @@
     own_q.start()
     own_l.start()
 
-    def send_kv(t, _):
-        to = lax.rem(me + t, N)
-        k_copy(me, to).start()
-        v_copy(me, to).start()
-        return 0
-
-    lax.fori_loop(1, N, send_kv, 0)
+    for dx, dc in MOVES:
+        for dy in (1, 0):
+            if (dy, dx, dc) != (0, 0, 0):
+                to = moved(me, dy, dx, dc)
+                k_copy(me, to).start()
+                v_copy(me, to).start()
 
     @pl.when(part == 0)
     def _():
@@ -185,25 +195,23 @@
     own_k.wait()
     own_v.wait()
 
-    @pl.when(part < N - 1)
-    def _():
-        halo_copy(me).start()
-
-    def forward(t, _):
-        slot = lax.rem(me + N - t, N)
-        k_copy(slot, me).wait_recv()
-        v_copy(slot, me).wait_recv()
-
+    def forward(dx, dc):
         @pl.when(part < N - 1)
         def _():
-            halo_copy(slot).start()
-
-        to = lax.rem(me + t, N)
-        q_copy(me, to).start()
-        l_copy(me, to).start()
-        return 0
-
-    lax.fori_loop(1, N, forward, 0)
+            for dy in (1, 0):
+                halo_copy(moved(me, dy, 4 - dx, dc)).start()
+
+    for at, (dx, dc) in enumerate(MOVES):
+        for dy in (1, 0):
+            if (dy, dx, dc) != (0, 0, 0):
+                slot = moved(me, dy, 4 - dx, dc)
+                k_copy(slot, me).wait_recv()
+                v_copy(slot, me).wait_recv()
+                to = moved(me, dy, dx, dc)
+                q_copy(me, to).start()
+                l_copy(me, to).start()
+        if at < len(MOVES) - HELD:
+            forward(dx, dc)
 
     def g1_copy(t):
         return remote(g1src.at[t], g1buf.at[part], g1_send.at[t], g1_recv.at[part], across(t))
@@ -254,21 +262,34 @@
         piece = jnp.where(holder == source, g1buf[source], piece)
     g2src[...] = piece
 
+    ring = (part // 8) * 8
+    opposite = lax.rem(part + 8, N)
+
     def g2_place(t):
         return gbuf.at[lax.rem(t, 2) * NGLOB + t // 2]
 
+    def in_ring(step):
+        return ring + lax.rem(part + step, 8)
+
     def g2_copy(slot, to):
         return remote(g2src, g2_place(slot), g2_send.at[to], g2_recv.at[slot], across(to))
 
+    def g2_cross(slot):
+        return remote(g2_place(slot), g2_place(slot), g2_over.at[slot], g2_recv.at[slot], across(opposite))
+
     own_g2 = pltpu.make_async_copy(g2src, g2_place(part), own_sem.at[1])
     own_g2.start()
-
-    def send_g2(t, _):
-        to = lax.rem(part + t, N)
-        g2_copy(part, to).start()
-        return 0
-
-    lax.fori_loop(1, N, send_g2, 0)
+    for step in FAR_FIRST:
+        g2_copy(part, in_ring(step)).start()
+
+    for dx, dc in MOVES[len(MOVES) - HELD :]:
+        forward(dx, dc)
+
+    own_g2.wait()
+    g2_cross(part).start()
+    for step in reversed(FAR_FIRST):
+        g2_copy(in_ring(step), part).wait_recv()
+        g2_cross(in_ring(step)).start()
 
     own_q.wait()
     own_l.wait()
@@ -284,13 +305,11 @@
     to_scalars.start()
     to_scalars.wait()
 
-    own_g2.wait()
-
     def wait_g2(t, _):
-        g2_copy(lax.rem(part + t, N), part).wait_recv()
+        g2_cross(8 - ring + t).wait_recv()
         return 0
 
-    lax.fori_loop(1, N, wait_g2, 0)
+    lax.fori_loop(0, 8, wait_g2, 0)
 
     def o_copy(group, source):
         columns = head_columns(out_ref, head_at(part, source))
@@ -300,40 +319,57 @@
 
     first = head_at(lax.rem(part + N - 1, N), head)
 
-    def came(slot):
-        return lax.rem(first + N - slot, N)
-
-    def ready(i):
-        last = came(i)
-        for back in (8, 4, 2, 1):
-            other = i + N - back
-            last = jnp.maximum(last, jnp.where(other < N, came(lax.rem(other, N)), 0))
-        return last
-
-    def step(t, _):
-        @pl.when(part > 0)
-        def _():
-            halo_copy(lax.rem(first + N - t, N)).wait_recv()
-
-        def group(i, _):
-            @pl.when(ready(i) == t)
-            def _():
-                obuf[i] = attend(part, i, qbuf, kv, lbs, gb_ref, gbuf)
-
-                @pl.when(i == me)
+    def groups(masked_far, masked_glob):
+        def step(n, _):
+            dx = sum(jnp.where(n == at, 4 - move[0], 0) for at, move in enumerate(MOVES))
+            dc = sum(jnp.where(n == at, move[1], 0) for at, move in enumerate(MOVES))
+            low = moved(first, 0, dx, dc)
+            low = jnp.where(low >= 8, low - 8, low)
+            pair = n < len(MOVES)
+
+            if not masked_far:
+
+                @pl.when(pair)
                 def _():
-                    own_o.start()
-
-                @pl.when(i != me)
+                    halo_copy(low + 8).wait_recv()
+                    halo_copy(low).wait_recv()
+
+            def group(half, _):
+                i = jnp.where(
+                    pair, low + 8 * (1 - half), lax.rem(me + 2 * (n - len(MOVES)) + half, 4)
+                )
+
+                @pl.when((half == 0) | (low >= 4) | (n >= len(MOVES)))
                 def _():
-                    o_copy(i, me).start()
-
+                    obuf[i] = attend(part, i, masked_far, masked_glob, qbuf, kv, lbs, gb_ref, gbuf)
+
+                    @pl.when(i == me)
+                    def _():
+                        own_o.start()
+
+                    @pl.when(i != me)
+                    def _():
+                        o_copy(i, me).start()
+
+                return 0
+
+            lax.fori_loop(0, 2, group, 0)
             return 0
 
-        lax.fori_loop(0, N, group, 0)
-        return 0
-
-    lax.fori_loop(0, N, step, 0)
+        lax.fori_loop(0, len(MOVES) + 2, step, 0)
+
+    @pl.when(part == 0)
+    def _():
+        groups(True, True)
+
+    @pl.when((part > 0) & (part < 4))
+    def _():
+        groups(False, True)
+
+    @pl.when(part >= 4)
+    def _():
+        groups(False, False)
+
     own_o.wait()
 
     def finish(t, _):
@@ -344,10 +380,13 @@
         l_copy(me, other).wait_send()
         o_copy(other, me).wait_send()
         o_copy(me, other).wait_recv()
-        g2_copy(part, lax.rem(part + t, N)).wait_send()
         return 0
 
     lax.fori_loop(1, N, finish, 0)
+    g2_cross(part).wait_send()
+    for step in FAR_FIRST:
+        g2_copy(part, in_ring(step)).wait_send()
+        g2_cross(in_ring(step)).wait_send()
 
     @pl.when(part < N - 1)
     def _():
@@ -368,16 +407,16 @@
 
 def shards(queries, keys, values, level_blocks, global_blocks):
     rows, width = queries.shape
-    levels = jnp.pad(level_blocks.reshape(1, -1), ((0, 7), (0, DH - level_blocks.size)))
     anywhere = pl.BlockSpec(memory_space=pl.ANY)
+    in_place = pl.BlockSpec(memory_space=pltpu.HBM)
     sems = pltpu.SemaphoreType.DMA
     return pl.pallas_call(
         kernel,
         out_shape=jax.ShapeDtypeStruct((rows, width), jnp.bfloat16),
         in_specs=[
-            anywhere,
-            anywhere,
-            anywhere,
+            in_place,
+            in_place,
+            in_place,
             pl.BlockSpec(memory_space=pltpu.VMEM),
             pl.BlockSpec(memory_space=pltpu.SMEM),
         ],
@@ -385,8 +424,8 @@
         scratch_shapes=[
             pltpu.VMEM((N, GRP, DH), jnp.bfloat16),
             pltpu.VMEM((2 * N, 2, GRP, DH), jnp.bfloat16),
-            pltpu.VMEM((N, 8, DH), jnp.int32),
-            pltpu.SMEM((N, 8, DH), jnp.int32),
+            pltpu.VMEM((N, 2, LEV), jnp.int32),
+            pltpu.SMEM((N, 2, LEV), jnp.int32),
             pltpu.VMEM((N, BLK, DH), jnp.bfloat16),
             pltpu.VMEM((4, BLK, DH), jnp.bfloat16),
             pltpu.VMEM((BLK, DH), jnp.bfloat16),
@@ -394,14 +433,14 @@
             pltpu.VMEM((N, GRP, DH), jnp.bfloat16),
         ]
         + [sems((N,))] * 8
-        + [sems((N,)), sems((N,)), sems((N,)), sems((4,)), sems((N,)), sems((N,)), sems((N,)), sems((N,)), sems((4,))],
+        + [sems((N,)), sems((N,)), sems((N,)), sems((4,)), sems((N,)), sems((N,)), sems((N,)), sems((N,)), sems((N,)), sems((4,))],
         compiler_params=pltpu.CompilerParams(
             collective_id=0, has_side_effects=True, vmem_limit_bytes=60 * 2**20
         ),
         cost_estimate=pl.CostEstimate(
             flops=4 * rows * width * 2048, bytes_accessed=8 * rows * width, transcendentals=rows * 2048 * N
         ),
-    )(queries, keys, values, levels, global_blocks)
+    )(queries, keys, values, level_blocks, global_blocks)
 
 
 def solution(mesh):

time: 129 us -> 109 us (0.84)
  Pallas kernels: 124 us -> 106 us
  local copies, waits for them, and re-layouts: 3.66 us -> 2.3 us
    pallas_call x1, Pallas kernels: 124 us -> 106 us  [shards(): pl.pallas_call(kernel, out_shape=jax.ShapeDtypeStruct((rows, width), jnp....]
where the time goes in v3:
time: 109 us; the launch traced here: 108 us
  Pallas kernels  106 us (97%)
  local copies, waits for them, and re-layouts  2.3 us (2%)
    pallas_call x1, Pallas kernels, shards(): pl.pallas_call(kernel, out_shape=jax.ShapeDtypeStruct((rows, width), jnp....  106 us
    unnamed x1, local copies, waits for them, and re-layouts  2.3 us

profile of v3, /device:TPU:17, one launch (start us, length us, event | category | flops | bytes accessed | tf_op | source)
XLA Modules:
  0.0 108.0 jit_solution(3277677509273646756)
XLA Ops:
  0.0 105.7 %shard_map.55 = bf16[256,2048]{1,0:T(8,128)(2,1)} custom-call(bf16[256,2048]{1,0:T(8,128)(2,1)} %q_ref.1, bf16[256,2048]{1,0:T(8,128)(2,1)} %k_ref.1, bf16[256,2048]{1,0:T(8,128)(2,1)} %v_ref.1, s32[2,4]{1,0:T(2,128)} %lb_ref.1, s32[8]{0:T(128)} %gb_ref.1), custom_call_target="tpu_custom_call" | custom-call | flops 4294967296 | bytes 4194304 | tf_op jit(solution)/shard_map/pallas_call | solution.py:413
  105.7 2.3 %copy.7 = bf16[256,2048]{1,0:T(8,128)(2,1)} copy(bf16[256,2048]{1,0:T(8,128)(2,1)} %shard_map.55) | data formatting | bytes 2097152

commit v4 on v3

--- a/solution.py
+++ b/solution.py
@@ -319,44 +319,43 @@
 
     first = head_at(lax.rem(part + N - 1, N), head)
 
+    def pair_low(n):
+        dx = sum(jnp.where(n == at, 4 - move[0], 0) for at, move in enumerate(MOVES))
+        dc = sum(jnp.where(n == at, move[1], 0) for at, move in enumerate(MOVES))
+        low = moved(first, 0, dx, dc)
+        return jnp.where(low >= 8, low - 8, low)
+
+    def send_out(i):
+        @pl.when(i == me)
+        def _():
+            own_o.start()
+
+        @pl.when(i != me)
+        def _():
+            o_copy(i, me).start()
+
     def groups(masked_far, masked_glob):
         def step(n, _):
-            dx = sum(jnp.where(n == at, 4 - move[0], 0) for at, move in enumerate(MOVES))
-            dc = sum(jnp.where(n == at, move[1], 0) for at, move in enumerate(MOVES))
-            low = moved(first, 0, dx, dc)
-            low = jnp.where(low >= 8, low - 8, low)
-            pair = n < len(MOVES)
+            upper = n < 4
+            lows = [pair_low(2 * n + k - jnp.where(upper, 0, 8)) for k in range(2)]
 
             if not masked_far:
 
-                @pl.when(pair)
+                @pl.when(upper)
                 def _():
-                    halo_copy(low + 8).wait_recv()
-                    halo_copy(low).wait_recv()
-
-            def group(half, _):
-                i = jnp.where(
-                    pair, low + 8 * (1 - half), lax.rem(me + 2 * (n - len(MOVES)) + half, 4)
-                )
-
-                @pl.when((half == 0) | (low >= 4) | (n >= len(MOVES)))
-                def _():
-                    obuf[i] = attend(part, i, masked_far, masked_glob, qbuf, kv, lbs, gb_ref, gbuf)
-
-                    @pl.when(i == me)
-                    def _():
-                        own_o.start()
-
-                    @pl.when(i != me)
-                    def _():
-                        o_copy(i, me).start()
-
-                return 0
-
-            lax.fori_loop(0, 2, group, 0)
+                    for low in lows:
+                        halo_copy(low + 8).wait_recv()
+                        halo_copy(low).wait_recv()
+
+            two = [low + jnp.where(upper, 8, 0) for low in lows]
+            made = [attend(part, i, masked_far, masked_glob, qbuf, kv, lbs, gb_ref, gbuf) for i in two]
+            for i, rows in zip(two, made):
+                obuf[i] = rows
+            for i in two:
+                send_out(i)
             return 0
 
-        lax.fori_loop(0, len(MOVES) + 2, step, 0)
+        lax.fori_loop(0, 8, step, 0)
 
     @pl.when(part == 0)
     def _():
@@ -435,12 +434,16 @@
         + [sems((N,))] * 8
         + [sems((N,)), sems((N,)), sems((N,)), sems((4,)), sems((N,)), sems((N,)), sems((N,)), sems((N,)), sems((N,)), sems((4,))],
         compiler_params=pltpu.CompilerParams(
-            collective_id=0, has_side_effects=True, vmem_limit_bytes=60 * 2**20
+            collective_id=0, has_side_effects=True, vmem_limit_bytes=40 * 2**20
         ),
         cost_estimate=pl.CostEstimate(
             flops=4 * rows * width * 2048, bytes_accessed=8 * rows * width, transcendentals=rows * 2048 * N
         ),
-    )(queries, keys, values, level_blocks, global_blocks)
+    )(
+        *[pltpu.with_memory_space_constraint(x, pltpu.HBM) for x in (queries, keys, values)],
+        level_blocks,
+        global_blocks,
+    )
 
 
 def solution(mesh):

time: 109 us -> 107 us (0.982)
  the two profiles are of different devices: /device:TPU:17 before, /device:TPU:1 now
where the time goes in v4:
time: 107 us
  Pallas kernels  104 us (97%)
  local copies, waits for them, and re-layouts  2.31 us (2%)
    pallas_call x1, Pallas kernels, shards(): pl.pallas_call(kernel, out_shape=jax.ShapeDtypeStruct((rows, width), jnp....  104 us
    unnamed x5, local copies, waits for them, and re-layouts  2.31 us

profile of v4, /device:TPU:1, one launch (start us, length us, event | category | flops | bytes accessed | tf_op | source)
XLA Modules:
  0.0 106.7 jit_solution(10659432476880048185)
XLA Ops:
  0.0 0.0 copy-start
  0.0 0.7 copy-done
  0.7 0.0 copy-start.1
  0.7 0.7 copy-done.1
  1.3 104.4 %shard_map.55 = bf16[256,2048]{1,0:T(8,128)(2,1)S(1)} custom-call(bf16[256,2048]{1,0:T(8,128)(2,1)} %q_ref.1, bf16[256,2048]{1,0:T(8,128)(2,1)} %k_ref.1, bf16[256,2048]{1,0:T(8,128)(2,1)} %v_ref.1, s32[2,4]{1,0:T(2,128)S(1)} %copy-done, s32[8]{0:T(128)S(1)} %copy-done.1), custom_call_target="tpu_custom_call" | custom-call | flops 4294967296 | bytes 4194304 | tf_op jit(solution)/shard_map/pallas_call | solution.py:412
  105.8 1.0 copy.7
Async XLA Ops:
  0.0 0.7 copy-start
  0.7 0.7 copy-start.1

commit v5 on v4

--- a/solution.py
+++ b/solution.py
@@ -18,6 +18,7 @@
 MASKED = -1e30
 MOVES = ((2, 0), (1, 0), (3, 1), (0, 0), (2, 1), (1, 1), (3, 0), (0, 1))
 HELD = 3
+WINDOW = 3
 FAR_FIRST = (4, 3, 5, 2, 6, 1, 7)
 SCALE_LOG2 = math.log2(math.e) / math.sqrt(DH)
 
@@ -172,12 +173,15 @@
     own_q.start()
     own_l.start()
 
-    for dx, dc in MOVES:
+    def send_pair(dx, dc):
         for dy in (1, 0):
             if (dy, dx, dc) != (0, 0, 0):
                 to = moved(me, dy, dx, dc)
                 k_copy(me, to).start()
                 v_copy(me, to).start()
+
+    for move in MOVES[:WINDOW]:
+        send_pair(*move)
 
     @pl.when(part == 0)
     def _():
@@ -207,11 +211,19 @@
                 slot = moved(me, dy, 4 - dx, dc)
                 k_copy(slot, me).wait_recv()
                 v_copy(slot, me).wait_recv()
+        if at + WINDOW < len(MOVES):
+            send_pair(*MOVES[at + WINDOW])
+        if at < len(MOVES) - HELD:
+            forward(dx, dc)
+        else:
+            pl.when(part >= 8)(functools.partial(forward, dx, dc))
+
+    for dx, dc in MOVES:
+        for dy in (1, 0):
+            if (dy, dx, dc) != (0, 0, 0):
                 to = moved(me, dy, dx, dc)
                 q_copy(me, to).start()
                 l_copy(me, to).start()
-        if at < len(MOVES) - HELD:
-            forward(dx, dc)
 
     def g1_copy(t):
         return remote(g1src.at[t], g1buf.at[part], g1_send.at[t], g1_recv.at[part], across(t))
@@ -283,7 +295,7 @@
         g2_copy(part, in_ring(step)).start()
 
     for dx, dc in MOVES[len(MOVES) - HELD :]:
-        forward(dx, dc)
+        pl.when(part < 8)(functools.partial(forward, dx, dc))
 
     own_g2.wait()
     g2_cross(part).start()

time: 107 us -> 106 us (level)
  the two profiles are of different devices: /device:TPU:1 before, /device:TPU:17 now
where the time goes in v5:
time: 106 us
  Pallas kernels  104 us (98%)
  local copies, waits for them, and re-layouts  2.31 us (2%)
    pallas_call x1, Pallas kernels, shards(): pl.pallas_call(kernel, out_shape=jax.ShapeDtypeStruct((rows, width), jnp....  104 us
    unnamed x5, local copies, waits for them, and re-layouts  2.31 us

profile of v5, /device:TPU:17, one launch (start us, length us, event | category | flops | bytes accessed | tf_op | source)
XLA Modules:
  0.0 106.0 jit_solution(8306954166534656824)
XLA Ops:
  0.0 0.0 copy-start
  0.0 0.7 copy-done
  0.7 0.0 copy-start.1
  0.7 0.7 copy-done.1
  1.3 103.7 %shard_map.55 = bf16[256,2048]{1,0:T(8,128)(2,1)S(1)} custom-call(bf16[256,2048]{1,0:T(8,128)(2,1)} %q_ref.1, bf16[256,2048]{1,0:T(8,128)(2,1)} %k_ref.1, bf16[256,2048]{1,0:T(8,128)(2,1)} %v_ref.1, s32[2,4]{1,0:T(2,128)S(1)} %copy-done, s32[8]{0:T(128)S(1)} %copy-done.1), custom_call_target="tpu_custom_call" | custom-call | flops 4294967296 | bytes 4194304 | tf_op jit(solution)/shard_map/pallas_call | solution.py:424
  105.0 1.0 copy.7
Async XLA Ops:
  0.0 0.7 copy-start
  0.7 0.7 copy-start.1

commit v6 on v5

--- a/solution.py
+++ b/solution.py
@@ -250,12 +250,8 @@
             g1src[2 * t + 1] = pick_v
         own_g1.start()
 
-        def send_g1(t, _):
-            g1_copy_to = lax.rem(part + t, N)
-            g1_copy(g1_copy_to).start()
-            return 0
-
-        lax.fori_loop(1, N, send_g1, 0)
+        for t in (4, 12, 3, 11, 5, 13, 2, 10, 6, 14, 1, 9, 7, 15, 8):
+            g1_copy(lax.rem(part + t, N)).start()
         own_g1.wait()
 
     def wait_g1(source, _):

time: 106 us -> 107 us (level)
  no operation moved by 1% of the time
where the time goes in v6:
time: 107 us
  Pallas kernels  104 us (97%)
  local copies, waits for them, and re-layouts  2.31 us (2%)
    pallas_call x1, Pallas kernels, shards(): pl.pallas_call(kernel, out_shape=jax.ShapeDtypeStruct((rows, width), jnp....  104 us
    unnamed x5, local copies, waits for them, and re-layouts  2.31 us

profile of v6, /device:TPU:17, one launch (start us, length us, event | category | flops | bytes accessed | tf_op | source)
XLA Modules:
  0.0 106.6 jit_solution(2603080242519870310)
XLA Ops:
  0.0 0.0 copy-start
  0.0 0.7 copy-done
  0.7 0.0 copy-start.1
  0.7 0.7 copy-done.1
  1.3 104.2 %shard_map.55 = bf16[256,2048]{1,0:T(8,128)(2,1)S(1)} custom-call(bf16[256,2048]{1,0:T(8,128)(2,1)} %q_ref.1, bf16[256,2048]{1,0:T(8,128)(2,1)} %k_ref.1, bf16[256,2048]{1,0:T(8,128)(2,1)} %v_ref.1, s32[2,4]{1,0:T(2,128)S(1)} %copy-done, s32[8]{0:T(128)S(1)} %copy-done.1), custom_call_target="tpu_custom_call" | custom-call | flops 4294967296 | bytes 4194304 | tf_op jit(solution)/shard_map/pallas_call | solution.py:420
  105.6 1.0 copy.7
Async XLA Ops:
  0.0 0.7 copy-start
  0.7 0.7 copy-start.1
